TPU v7x, 32 devices: a whole 2x2x4 slice. The times are simulated.
32 devices in a mesh: dp: 8 (over z, y), mp: 4 (over x, core).
Axes of the slice: x: 2, y: 2, z: 4, core: 2. Of those that a mesh axis runs over, the one named last changes fastest.
Arguments:
- embeddings: bfloat16 [2048, 768], P('dp'), may hold values from -8192 to 8192
- cluster_ids: int32 [2048], P('dp'), may hold values from 0 to 31, as said below
Outputs:
- scores: float32 [2048], P('dp')
Inputs may be any that keep to these rules, and one draw needn't show every extreme that they name: `cluster_ids`: the owner of cluster c is the index c // 4 of dp. Of the 256 rows of one index of dp, at most 64 lie in the clusters of one owner, and some owner gets exactly 64 rows from every index of dp.
All inputs are finite; a program needn't handle non-finite values.
Results may differ from a plain program's by a relative error of at most 0.0018.
Values may be sent and summed in bfloat16 or wider, within the bound.
No kernel may reach another device: no remote copies, remote signals or barrier semaphores. Data moves between devices by JAX's collectives and lax.ppermute only.
A program may use at most 64 MiB of HBM per device.

v0:
```python
import functools
import jax
import jax.numpy as jnp
from jax import lax
from jax.experimental import pallas as pl
from jax.experimental.pallas import tpu as pltpu
from jax.sharding import PartitionSpec as P

CPO = 4
GATHER_LIMIT = 8 * 1024 * 1024
BLK = 128
SUB = 8
GROUP = 4
PANEL = 256


def refine(value):
    guess = pl.reciprocal(value, approx=True)
    return guess * (2.0 - value * guess)


def invert_factor(block, jobs):
    shape = (SUB, BLK)
    lane = lax.broadcasted_iota(jnp.int32, shape, 1)
    sub = lax.broadcasted_iota(jnp.int32, shape, 0)
    count = BLK // SUB
    slots = count * SUB // 2
    jobs = list(jobs)
    total = len(jobs)
    rows = [block[SUB * i : SUB * (i + 1), :] for i in range(count)]

    def spread(i, at):
        return [jnp.broadcast_to(rows[i][:, at + q : at + q + 1], shape) for q in range(SUB)]

    def line(value, p):
        return jnp.broadcast_to(value[p : p + 1, :], shape)

    def follow(i, first, steps):
        cols = spread(i, first)
        value = jnp.where((lane >= first) & (lane < first + SUB), 0.0, rows[i])
        for p, (inverse, tops, pivot_row) in enumerate(steps):
            factor = cols[p] * inverse
            for q in range(p + 1, SUB):
                cols[q] = cols[q] - factor * tops[q]
            value = value - factor * pivot_row
        rows[i] = value

    def follow_group(end, members):
        start = end - SUB * GROUP
        factors = as_right(split(jnp.concatenate(members, axis=0)), 0)
        lines = [
            jnp.where((lane >= start + SUB * (n + 1)) & (lane < end), 0.0, member) for n, member in enumerate(members)
        ]
        a, b, c = split(jnp.concatenate(lines, axis=0))
        change = lax.dot_general(
            factors,
            jnp.concatenate([a, a, b, b, a, c], axis=0),
            (((0,), (0,)), ((), ())),
            preferred_element_type=jnp.float32,
        )
        for i in range(end // SUB + GROUP, count):
            kept = jnp.where((lane >= start) & (lane < end), 0.0, rows[i])
            rows[i] = kept - change[SUB * i : SUB * (i + 1), :]

    done = []
    late = []
    members = []
    cols = spread(0, 0)
    for t in range(count):
        first = SUB * t
        here = (lane >= first) & (lane < first + SUB)
        window = min((t // GROUP + 2) * GROUP, count)
        every = {i: spread(i, first) for i in range(t + 1, min(t + 3, window))}
        if every:
            ahead = spread(t, first + SUB)
            next_cols = spread(t + 1, first + SUB)
        late_total = len(late)
        steps = []
        rows[t] = jnp.where(here, (lane - first == sub).astype(jnp.float32), rows[t])
        for i in every:
            rows[i] = jnp.where(here, 0.0, rows[i])
        pivots = jnp.ones(shape, jnp.float32)
        for p in range(0, SUB, 2):
            first_pivot, cross = line(cols[p], p), line(cols[p + 1], p)
            cross_low, corner = line(cols[p], p + 1), line(cols[p + 1], p + 1)
            det = first_pivot * corner - cross * cross_low
            inv1 = refine(first_pivot)
            guess = pl.reciprocal(det, approx=True)
            inv2 = (first_pivot * guess) * (2.0 - det * guess)
            below1 = jnp.where(sub > p, cols[p], 0.0)
            factor1 = below1 * inv1
            factor2 = jnp.where(sub > p + 1, cols[p + 1] - (below1 * cross) * inv1, 0.0) * inv2
            top1 = {q: line(cols[q], p) for q in range(p + 2, SUB)}
            top2 = {q: line(cols[q], p + 1) - (cross_low * top1[q]) * inv1 for q in range(p + 2, SUB)}
            for q in range(p + 2, SUB):
                cols[q] = (cols[q] - factor1 * top1[q]) - factor2 * top2[q]
            low = cross_low * inv1
            row1 = line(rows[t], p)
            row2 = line(rows[t], p + 1) - low * row1
            rows[t] = (rows[t] - factor1 * row1) - factor2 * row2
            pivots = jnp.where(sub == p, first_pivot, jnp.where(sub == p + 1, det * inv1, pivots))
            top1[p + 1] = cross
            steps += [(inv1, top1, row1), (inv2, top2, row2)]
            if every:
                ahead1 = [line(value, p) for value in ahead]
                ahead2 = [line(value, p + 1) - low * one for value, one in zip(ahead, ahead1)]
                ahead = [(v - factor1 * one) - factor2 * two for v, one, two in zip(ahead, ahead1, ahead2)]
            for i, values in every.items():
                near1 = values[p] * inv1
                near2 = (values[p + 1] - near1 * cross) * inv2
                for q in range(p + 2, SUB):
                    values[q] = (values[q] - near1 * top1[q]) - near2 * top2[q]
                rows[i] = (rows[i] - near1 * row1) - near2 * row2
                if i == t + 1:
                    next_cols = [
                        (v - near1 * one) - near2 * two for v, one, two in zip(next_cols, ahead1, ahead2)
                    ]
            for _ in range(late_total * (p + 2) // SUB - late_total * p // SUB):
                late.pop(0)()
            slot = (t * SUB + p) // 2
            for job in jobs[total * slot // slots : total * (slot + 1) // slots]:
                job()
        scale = lax.rsqrt(pivots)
        scale = scale * (1.5 - 0.5 * pivots * scale * scale)
        scaled = rows[t] * scale
        done.append(jnp.where(lane <= first + sub, scaled, 0.0))
        if every:
            cols = next_cols
        if t + 3 < window:
            follow(t + 3, first, steps)
        late += [functools.partial(follow, i, first, steps) for i in range(t + 4, window)]
        members.append(scaled)
        if len(members) == GROUP:
            if window < count:
                follow_group(first + SUB, members)
            members = []
    return jnp.concatenate(done, axis=0)


def dot_nn(a, b):
    return lax.dot_general(a, b, (((1,), (0,)), ((), ())), preferred_element_type=jnp.float32)


def dot_nt(a, b):
    return lax.dot_general(a, b, (((1,), (1,)), ((), ())), preferred_element_type=jnp.float32)


def split(value):
    high = value.astype(jnp.bfloat16)
    rest = value - high.astype(jnp.float32)
    mid = rest.astype(jnp.bfloat16)
    return high, mid, (rest - mid.astype(jnp.float32)).astype(jnp.bfloat16)


def as_left(terms):
    a, b, c = terms
    return jnp.concatenate([a, a, b, b, a, c], axis=1)


def as_right(terms, axis):
    a, b, c = terms
    return jnp.concatenate([a, b, a, b, c, a], axis=axis)


def score_kernel(sizes, *refs):
    pieces = refs[: len(sizes)]
    ids_ref, out_ref = refs[len(sizes) : len(sizes) + 2]
    rows, flipped, work, left, right, below, white, own_white, sims, sums = refs[len(sizes) + 2 :]
    row_total, width = rows.shape
    own = sizes[0]
    count = width // BLK
    blocks = [slice(BLK * n, BLK * (n + 1)) for n in range(count)]
    chunks = [slice(n, n + 2 * own) for n in range(0, row_total, 2 * own)]

    at = 0
    for size, source in zip(sizes, pieces):
        rows[at : at + size, :] = source[...]
        at += size

    def flip_columns(at, size):
        flipped[at : at + size, :] = rows[:, at : at + size].T

    def moments_of(at, size, to, to_size):
        mean = dot_nn(flipped[at : at + size, :], rows[:, to : to + to_size]) * (1.0 / row_total)
        if at < to + to_size:
            shape = (size, to_size)
            row_i = at + lax.broadcasted_iota(jnp.int32, shape, 0)
            col_i = to + lax.broadcasted_iota(jnp.int32, shape, 1)
            mean = mean + jnp.where(row_i == col_i, 0.001, 0.0)
        work[at : at + size, to : to + to_size] = mean

    def mask_of(at):
        own_col = jnp.broadcast_to(ids_ref[:, 0:own], (BLK, own)).T[:, 0:1]
        same = own_col == ids_ref[:, at : at + BLK]
        if at < own:
            own_pos = lax.broadcasted_iota(jnp.int32, (own, BLK), 0)
            same = same & (own_pos != at + lax.broadcasted_iota(jnp.int32, (own, BLK), 1))
        sims[:, at : at + BLK] = jnp.where(same, 0.0, -1e30)

    def first_jobs():
        jobs = [functools.partial(flip_columns, BLK, PANEL - BLK)]
        jobs.append(functools.partial(moments_of, BLK, PANEL - BLK, 0, PANEL))
        jobs += [functools.partial(flip_columns, at, PANEL) for at in range(PANEL, width, PANEL)]
        for to in range(0, width, PANEL):
            at = max(to, PANEL)
            jobs.append(functools.partial(moments_of, at, width - at, to, PANEL))
        return jobs + [functools.partial(mask_of, at) for at in range(0, row_total, BLK)]

    def left_of(begin, h, inverse_right):
        terms = split(dot_nt(as_left(split(work[begin:width, blocks[h]])), inverse_right))
        left[begin:width, :] = as_left(terms)
        right[begin:width, :] = as_right(terms, 1)

    def below_of(h, inverse_left):
        known = slice(0, BLK * h)
        value = dot_nn(inverse_left, as_right(split(work[blocks[h], known]), 0))
        below[:, known] = as_right(split(value), 0)
        white[blocks[h % 4], known] = value.astype(jnp.bfloat16)

    def reduce_left(begin, h):
        known = slice(0, BLK * (h + 1))
        work[begin:width, blocks[h]] = jnp.zeros((width - begin, BLK), jnp.float32)
        work[begin:width, known] -= dot_nn(left[begin:width, :], below[:, known])

    def reduce_right(begin, size):
        work[begin:width, begin : begin + size] -= dot_nt(left[begin:width, :], right[begin : begin + size, :])

    def whiten_own(h, begin, size):
        feats = slice(0, BLK * (h + 1))
        own_white[:, 0:size] = dot_nt(rows[0:own, feats], white[begin : begin + size, feats]).astype(jnp.bfloat16)

    def whiten(c, h, begin, size):
        feats = slice(0, BLK * (h + 1))
        whitened = dot_nt(white[begin : begin + size, feats], rows[chunks[c], feats]).astype(jnp.bfloat16)
        sims[:, chunks[c]] += dot_nn(own_white[:, 0:size], whitened)
        widened = whitened.astype(jnp.float32)
        squares = sum(widened[n : n + SUB, :] * widened[n : n + SUB, :] for n in range(0, size, SUB))
        sums[:, chunks[c]] = squares if h < 2 else sums[:, chunks[c]] + squares

    def whiten_jobs(h, begin, size):
        jobs = [functools.partial(whiten_own, h, begin, size)]
        return jobs + [functools.partial(whiten, c, h, begin, size) for c in range(len(chunks))]

    def finish_rows(h, inverse):
        white[blocks[h % 4], blocks[h]] = inverse.astype(jnp.bfloat16)
        terms = split(inverse)
        below[:, blocks[h]] = as_right(terms, 0)
        jobs = [functools.partial(below_of, h, as_left(terms))] if h else []
        if h >= count - 2:
            return jobs, whiten_jobs(h, BLK * (h % 4), BLK)
        if h % 2 == 0:
            white[blocks[h % 4], blocks[h + 1]] = jnp.zeros((BLK, BLK), jnp.bfloat16)
            return jobs, []
        return jobs, whiten_jobs(h, BLK * (h % 4 - 1), 2 * BLK)

    flip_columns(0, BLK)
    moments_of(0, BLK, 0, BLK)
    block = work[blocks[0], blocks[0]]
    jobs = first_jobs()
    waiting = []
    for k in range(count):
        inverse = invert_factor(block, jobs)
        jobs, white_jobs = finish_rows(k, inverse)
        if k + 1 == count:
            break
        terms = split(inverse)
        inverse_right = as_right(terms, 1)
        nexts = blocks[k + 1]
        terms = split(dot_nt(as_left(split(work[nexts, blocks[k]])), inverse_right))
        value_left, value_right = as_left(terms), as_right(terms, 1)
        block = work[nexts, nexts] - dot_nt(value_left, value_right)
        left[nexts, :] = value_left
        right[nexts, :] = value_right
        begin = BLK * (k + 1)
        if begin + BLK < width:
            jobs.append(functools.partial(left_of, begin + BLK, k, inverse_right))
            for at in range(begin, width, PANEL):
                jobs.append(functools.partial(reduce_right, at, min(PANEL, width - at)))
        jobs.append(functools.partial(reduce_left, begin, k))
        if k % 2 == 1 and white_jobs:
            waiting = white_jobs[len(white_jobs) // 2 :]
            jobs += white_jobs[: len(white_jobs) // 2]
        else:
            jobs += waiting + white_jobs
            waiting = []
    for job in jobs + white_jobs:
        job()

    key_sums = jnp.sum(sums[...], axis=0, keepdims=True)
    scales = lax.rsqrt(key_sums + 1e-06)
    best = jnp.full((own, BLK), -1e30, jnp.float32)
    for at in range(0, row_total, BLK):
        best = jnp.maximum(best, sims[:, at : at + BLK] * scales[:, at : at + BLK])
    top = jnp.max(best, axis=1, keepdims=True)
    own_scale = jnp.broadcast_to(scales[:, 0:own], (BLK, own)).T[:, 0:1]
    top = jnp.where(top < -1e20, -1.0, jnp.maximum(top * own_scale, -1.0))
    out_ref[...] = jnp.broadcast_to(top, (own, BLK)).T[0:1, :]


def scores_of(pieces, ids):
    sizes = tuple(piece.shape[0] for piece in pieces)
    row_total, width, own = sum(sizes), pieces[0].shape[1], sizes[0]
    vmem = pl.BlockSpec(memory_space=pltpu.VMEM)
    out = pl.pallas_call(
        functools.partial(score_kernel, sizes),
        out_shape=jax.ShapeDtypeStruct((1, own), jnp.float32),
        in_specs=[vmem] * (len(sizes) + 1),
        out_specs=vmem,
        scratch_shapes=[
            pltpu.VMEM((row_total, width), jnp.bfloat16),
            pltpu.VMEM((width, row_total), jnp.bfloat16),
            pltpu.VMEM((width, width), jnp.float32),
            pltpu.VMEM((width, 6 * BLK), jnp.bfloat16),
            pltpu.VMEM((width, 6 * BLK), jnp.bfloat16),
            pltpu.VMEM((6 * BLK, width), jnp.bfloat16),
            pltpu.VMEM((4 * BLK, width), jnp.bfloat16),
            pltpu.VMEM((own, 2 * BLK), jnp.bfloat16),
            pltpu.VMEM((own, row_total), jnp.float32),
            pltpu.VMEM((SUB, row_total), jnp.float32),
        ],
        compiler_params=pltpu.CompilerParams(vmem_limit_bytes=32 * 1024 * 1024),
    )(*pieces, ids.reshape(1, -1))
    return out.reshape(own)


def contract_rows(left_rows, right_rows):
    return lax.dot_general(
        left_rows, right_rows, (((0,), (0,)), ((), ())), preferred_element_type=jnp.float32
    )


def normalize_rows(values):
    widened = values.astype(jnp.float32)
    square_sum = jnp.sum(widened * widened, axis=1, keepdims=True)
    inverse_norm = lax.rsqrt(square_sum + 1e-06)
    return (widened * inverse_norm).astype(jnp.bfloat16)


def best_match(queries, query_ids, query_start, key_units, key_ids):
    similarity = lax.dot_general(
        queries, key_units, (((1,), (1,)), ((), ())), preferred_element_type=jnp.float32
    )
    query_pos = query_start + jnp.arange(queries.shape[0], dtype=jnp.int32)
    key_pos = jnp.arange(key_units.shape[0], dtype=jnp.int32)
    same_cluster = (
        (query_ids[:, None] == key_ids[None, :])
        & (query_ids[:, None] >= 0)
        & (query_pos[:, None] != key_pos[None, :])
    )
    return jnp.max(jnp.where(same_cluster, similarity, -1.0), axis=1)


def whitening_of(moments, row_total):
    identity = jnp.eye(moments.shape[0], dtype=jnp.float32)
    chol_factor = jnp.linalg.cholesky(moments / float(row_total) + 0.001 * identity)
    return jax.scipy.linalg.solve_triangular(chol_factor, identity, lower=True).astype(
        jnp.bfloat16
    )


def exchange(value, axis, flip):
    return lax.ppermute(value, axis, [(i, i ^ flip) for i in range(lax.axis_size(axis))])


def local_gathered(embeddings, cluster_ids):
    row_count = embeddings.shape[0]
    dp_count = lax.axis_size("dp")
    mp_index = lax.axis_index("mp")
    core, side = mp_index % 2, mp_index // 2
    half, quarter = row_count // 2, row_count // 4

    own_half = lax.dynamic_slice_in_dim(embeddings, core * half, half, 0)
    own_quarter = lax.dynamic_slice_in_dim(own_half, side * quarter, quarter, 0)
    far = jnp.concatenate([exchange(own_quarter, "dp", flip) for flip in range(4, dp_count, 2)], axis=0)
    zone = exchange(own_half, "dp", 2)
    near = exchange(own_half, "dp", 1)
    ids = cluster_ids[None]
    next_ids = exchange(ids, "dp", 2)
    far, near, next_ids = lax.optimization_barrier((far, near, next_ids))

    far_near = exchange(far, "dp", 1)
    far_side = exchange(far, "mp", 2)
    zone_near = exchange(zone, "dp", 1)
    ids = jnp.concatenate([ids, next_ids], axis=0)
    ids = jnp.concatenate([ids, exchange(ids, "dp", 4)], axis=0)
    far_near_side = exchange(far_near, "mp", 2)

    ids = jnp.concatenate([ids, exchange(ids, "dp", 1)], axis=0)
    place = {0: 0, 2: 1, 4: 2, 6: 3, 1: 4, 3: 5, 5: 6, 7: 7}

    held = lax.optimization_barrier([near, zone, zone_near, far, far_side, far_near, far_near_side])
    pieces = [embeddings] + held + [exchange(value, "mp", 1) for value in held]

    def ids_of(sources, start, size):
        return [lax.dynamic_slice_in_dim(ids[place[n]], start, size, 0) for n in sources]

    orders = [cluster_ids]
    for c in (core, 1 - core):
        orders += ids_of((1, 2, 3), c * half, half)
        for first in (4, 5):
            for s in (side, 1 - side):
                orders += ids_of(range(first, dp_count, 2), c * half + s * quarter, quarter)
    return scores_of(pieces, jnp.concatenate(orders))


def local_routed(embeddings, cluster_ids):
    row_count, feat_width = embeddings.shape
    dp_count = lax.axis_size("dp")
    mp_count = lax.axis_size("mp")
    mp_index = lax.axis_index("mp")
    pair_cap = 2 * row_count // dp_count
    slot_count = dp_count * pair_cap
    quarter_len = slot_count // mp_count
    col_share = feat_width // mp_count
    own_cols = lax.dynamic_slice_in_dim(embeddings, mp_index * col_share, col_share, 1)
    column_sums = lax.psum(contract_rows(embeddings, own_cols), "dp")
    moments = lax.all_gather(column_sums, "mp", axis=1, tiled=True)
    whitening = whitening_of(moments, row_count * dp_count)
    owner_ids = cluster_ids // CPO
    owner_hits = (owner_ids[:, None] == jnp.arange(dp_count, dtype=jnp.int32)[None, :]).astype(
        jnp.int32
    )
    earlier_hits = jnp.cumsum(owner_hits, axis=0) - owner_hits
    row_rank = jnp.sum(earlier_hits * owner_hits, axis=1)
    whiten_part = lax.dynamic_slice_in_dim(whitening, mp_index * col_share, col_share, 0)
    whitened = lax.dot_general(
        embeddings, whiten_part, (((1,), (1,)), ((), ())), preferred_element_type=jnp.float32
    ).astype(jnp.bfloat16)
    slot_index = owner_ids * pair_cap + row_rank
    send_rows = jnp.zeros((slot_count, col_share), jnp.bfloat16).at[slot_index].set(whitened)
    send_ids = jnp.full((slot_count,), -1, jnp.int32).at[slot_index].set(cluster_ids)
    got_rows, got_ids = (
        lax.all_to_all(send_rows, "dp", split_axis=0, concat_axis=0, tiled=True),
        lax.all_to_all(send_ids, "dp", split_axis=0, concat_axis=0, tiled=True),
    )
    key_rows = lax.all_gather(got_rows, "mp", axis=1, tiled=True)
    unit = normalize_rows(key_rows)
    query_start = mp_index * quarter_len
    queries = lax.dynamic_slice_in_dim(unit, query_start, quarter_len, 0)
    query_ids = lax.dynamic_slice_in_dim(got_ids, query_start, quarter_len, 0)
    best_score = best_match(queries, query_ids, query_start, unit, got_ids)
    all_scores = lax.all_gather(best_score, "mp", axis=0, tiled=True)
    returned = lax.all_to_all(all_scores, "dp", split_axis=0, concat_axis=0, tiled=True)
    return returned[slot_index]


def local(embeddings, cluster_ids):
    owners = lax.axis_size("dp")
    fits = embeddings.size * 2 * owners <= GATHER_LIMIT
    if fits and lax.axis_size("mp") == 4 and owners == 8:
        return local_gathered(embeddings, cluster_ids)
    return local_routed(embeddings, cluster_ids)


def solution(mesh):
    in_specs = (P("dp", None), P("dp"))
    out_specs = P("dp")
    return jax.shard_map(local, mesh=mesh, in_specs=in_specs, out_specs=out_specs, check_vma=False)
```

profile of v0, /device:TPU:0, one launch (start us, length us, event | category | flops | bytes accessed | tf_op | source)
XLA Modules:
  0.0 60.5 jit_solution(7122357005191940182)
XLA Ops:
  0.0 0.9 %constant_dynamic-slice_fusion.23 = bf16[64,768]{1,0:T(8,128)(2,1)S(1)} fusion(bf16[256,768]{1,0:T(8,128)(2,1)} %refs_0_.1, s32[]{:T(128)S(6)} %dynamic_slice.119), kind=kLoop, calls=%fused_computation.24 | loop fusion | bytes 196612 | tf_op jit(solution)/shard_map/dynamic_slice | solution.py:373
  0.9 5.1 %collective-permute-start.1 = (bf16[64,768]{1,0:T(8,128)(2,1)S(1)}, bf16[64,768]{1,0:T(8,128)(2,1)S(1)}, u32[]{:S(2)}, u32[]{:S(2)}) collective-permute-start(bf16[64,768]{1,0:T(8,128)(2,1)S(1)} %constant_dynamic-slice_fusion.23), channel_id=1, source_target_pairs={{0,24},{4,28},{8,16},{12,20},{16,8},{20,12},{24,0},{28,4},{1,25},{... | collective-permute-start | bytes 294920 | tf_op jit(solution)/shard_map/ppermute | solution.py:362
  6.1 0.9 %constant_dynamic-slice_fusion.22 = bf16[128,768]{1,0:T(8,128)(2,1)S(1)} fusion(bf16[256,768]{1,0:T(8,128)(2,1)} %refs_0_.1, s32[]{:T(128)S(6)} %select_n.57), kind=kLoop, calls=%fused_computation.23 | loop fusion | bytes 393220 | tf_op jit(solution)/shard_map/dynamic_slice | solution.py:372
  7.0 1.6 %collective-permute-start.2 = (bf16[128,768]{1,0:T(8,128)(2,1)S(1)}, bf16[128,768]{1,0:T(8,128)(2,1)S(1)}, u32[]{:S(2)}, u32[]{:S(2)}) collective-permute-start(bf16[128,768]{1,0:T(8,128)(2,1)S(1)} %constant_dynamic-slice_fusion.22), channel_id=1, source_target_pairs={{0,4},{4,0},{8,12},{12,8},{16,20},{20,16},{24,28},{28,24},{1,5},{5... | collective-permute-start | bytes 589832 | tf_op jit(solution)/shard_map/ppermute | solution.py:362
  8.6 0.8 %collective-permute-start.4 = (bf16[128,768]{1,0:T(8,128)(2,1)S(1)}, bf16[128,768]{1,0:T(8,128)(2,1)S(1)}, u32[]{:S(2)}, u32[]{:S(2)}) collective-permute-start(bf16[128,768]{1,0:T(8,128)(2,1)S(1)} %constant_dynamic-slice_fusion.22), channel_id=1, source_target_pairs={{0,8},{4,12},{8,0},{12,4},{16,24},{20,28},{24,16},{28,20},{1,9},{5... | collective-permute-start | bytes 589832 | tf_op jit(solution)/shard_map/ppermute | solution.py:362
  9.4 1.2 %collective-permute-start.3 = (s32[1,256]{1,0:T(1,128)S(1)}, s32[1,256]{1,0:T(1,128)S(1)}, u32[]{:S(2)}, u32[]{:S(2)}) collective-permute-start(s32[1,256]{1,0:T(1,128)S(1)} %bitcast.48), channel_id=1, source_target_pairs={{0,8},{4,12},{8,0},{12,4},{16,24},{20,28},{24,16},{28,20},{1,9},{5... | collective-permute-start | bytes 3080 | tf_op jit(solution)/shard_map/ppermute | solution.py:362
  10.6 3.8 %collective-permute-done = bf16[64,768]{1,0:T(8,128)(2,1)S(1)} collective-permute-done((bf16[64,768]{1,0:T(8,128)(2,1)S(1)}, bf16[64,768]{1,0:T(8,128)(2,1)S(1)}, u32[]{:S(2)}, u32[]{:S(2)}) %collective-permute-start) | collective-permute-done | bytes 98336 | tf_op jit(solution)/shard_map/ppermute | solution.py:362
  14.4 2.4 %collective-permute-done.3 = s32[1,256]{1,0:T(1,128)S(1)} collective-permute-done((s32[1,256]{1,0:T(1,128)S(1)}, s32[1,256]{1,0:T(1,128)S(1)}, u32[]{:S(2)}, u32[]{:S(2)}) %collective-permute-start.3) | collective-permute-done | bytes 1056 | tf_op jit(solution)/shard_map/ppermute | solution.py:362
  16.8 0.7 %collective-permute-start.7 = (bf16[128,768]{1,0:T(8,128)(2,1)S(1)}, bf16[128,768]{1,0:T(8,128)(2,1)S(1)}, u32[]{:S(2)}, u32[]{:S(2)}) collective-permute-start(bf16[128,768]{1,0:T(8,128)(2,1)S(1)} %pad_maximum_fusion.refs_4_), channel_id=1, source_target_pairs={{0,4},{4,0},{8,12},{12,8},{16,20},{20,16},{24,28},{28,24},{1,5},{5... | collective-permute-start | bytes 589832 | tf_op jit(solution)/shard_map/ppermute | solution.py:362
  17.5 1.5 %collective-permute-start.6 = (bf16[128,768]{1,0:T(8,128)(2,1)S(1)}, bf16[128,768]{1,0:T(8,128)(2,1)S(1)}, u32[]{:S(2)}, u32[]{:S(2)}) collective-permute-start(bf16[128,768]{1,0:T(8,128)(2,1)S(1)} %pad_maximum_fusion.refs_4_), channel_id=1, source_target_pairs={{0,2},{1,3},{2,0},{3,1},{4,6},{5,7},{6,4},{7,5},{8,10},{9,11},{10,... | collective-permute-start | bytes 589832 | tf_op jit(solution)/shard_map/ppermute | solution.py:362
  19.0 0.7 %collective-permute-start.16 = (s32[2,256]{1,0:T(2,128)S(1)}, s32[2,256]{1,0:T(2,128)S(1)}, u32[]{:S(2)}, u32[]{:S(2)}) collective-permute-start(s32[2,256]{1,0:T(2,128)S(1)} %pad_add_fusion.1), channel_id=1, source_target_pairs={{0,16},{4,20},{8,24},{12,28},{16,0},{20,4},{24,8},{28,12},{1,17},{... | collective-permute-start | bytes 6152 | tf_op jit(solution)/shard_map/ppermute | solution.py:362
  19.7 1.2 %collective-permute-start.5 = (bf16[128,768]{1,0:T(8,128)(2,1)S(1)}, bf16[128,768]{1,0:T(8,128)(2,1)S(1)}, u32[]{:S(2)}, u32[]{:S(2)}) collective-permute-start(bf16[128,768]{1,0:T(8,128)(2,1)S(1)} %collective-permute-done.4.refs_2_), channel_id=1, source_target_pairs={{0,4},{4,0},{8,12},{12,8},{16,20},{20,16},{24,28},{28,24},{1,5},{5... | collective-permute-start | bytes 589832 | tf_op jit(solution)/shard_map/ppermute | solution.py:362
  20.9 2.6 %collective-permute-done.16 = s32[2,256]{1,0:T(2,128)S(1)} collective-permute-done((s32[2,256]{1,0:T(2,128)S(1)}, s32[2,256]{1,0:T(2,128)S(1)}, u32[]{:S(2)}, u32[]{:S(2)}) %collective-permute-start.16) | collective-permute-done | bytes 2080 | tf_op jit(solution)/shard_map/ppermute | solution.py:362
  23.5 1.4 %collective-permute-start.17 = (s32[4,256]{1,0:T(4,128)S(1)}, s32[4,256]{1,0:T(4,128)S(1)}, u32[]{:S(2)}, u32[]{:S(2)}) collective-permute-start(s32[4,256]{1,0:T(4,128)S(1)} %pad_add_fusion), channel_id=1, source_target_pairs={{0,4},{4,0},{8,12},{12,8},{16,20},{20,16},{24,28},{28,24},{1,5},{5... | collective-permute-start | bytes 12296 | tf_op jit(solution)/shard_map/ppermute | solution.py:362
  24.9 1.1 %collective-permute-start.8 = (bf16[128,768]{1,0:T(8,128)(2,1)S(1)}, bf16[128,768]{1,0:T(8,128)(2,1)S(1)}, u32[]{:S(2)}, u32[]{:S(2)}) collective-permute-start(bf16[128,768]{1,0:T(8,128)(2,1)S(1)} %collective-permute-done.7.refs_6_), channel_id=1, source_target_pairs={{0,2},{1,3},{2,0},{3,1},{4,6},{5,7},{6,4},{7,5},{8,10},{9,11},{10,... | collective-permute-start | bytes 589832 | tf_op jit(solution)/shard_map/ppermute | solution.py:362
  26.1 0.1 fusion.16
  26.1 0.6 %collective-permute-done.5.refs_3_ = bf16[128,768]{1,0:T(8,128)(2,1)S(1)} collective-permute-done((bf16[128,768]{1,0:T(8,128)(2,1)S(1)}, bf16[128,768]{1,0:T(8,128)(2,1)S(1)}, u32[]{:S(2)}, u32[]{:S(2)}) %collective-permute-start.5) | collective-permute-done | bytes 196640 | tf_op jit(solution)/shard_map/ppermute | solution.py:362
  26.8 3.8 %collective-permute-done.8.refs_7_ = bf16[128,768]{1,0:T(8,128)(2,1)S(1)} collective-permute-done((bf16[128,768]{1,0:T(8,128)(2,1)S(1)}, bf16[128,768]{1,0:T(8,128)(2,1)S(1)}, u32[]{:S(2)}, u32[]{:S(2)}) %collective-permute-start.8) | collective-permute-done | bytes 196640 | tf_op jit(solution)/shard_map/ppermute | solution.py:362
  30.6 0.5 collective-permute-start.10
  31.2 0.5 collective-permute-start.12
  31.7 0.1 collective-permute-start.13
  31.8 0.3 collective-permute-done.9.refs_8_
  32.0 0.2 collective-permute-start.14
  32.2 0.1 collective-permute-done.10.refs_9_
  32.3 0.2 collective-permute-start.15
  32.6 0.1 fusion.20
  32.6 0.1 concatenate.16
  32.7 0.2 collective-permute-done.12.refs_11_
  32.9 0.3 collective-permute-done.13.refs_12_
  33.2 0.3 collective-permute-done.14.refs_13_
  33.5 0.3 collective-permute-done.15.refs_14_
  33.8 26.7 %shard_map.28 = f32[1,256]{1,0:T(1,128)} custom-call(bf16[256,768]{1,0:T(8,128)(2,1)S(1)} %copy-done, bf16[128,768]{1,0:T(8,128)(2,1)S(1)} %collective-permute-done.2.refs_1_, bf16[128,768]{1,0:T(8,128)(2,1)S(1)} %collective-permute-done.4.refs_2_, bf16[128,768]{1,0:T(8,128)(2,1)S(1)} %collective-permute-done.5.refs_3_, ...), custom_call_target="tpu_custom_call" | custom-call | tf_op jit(solution)/shard_map/pallas_call | solution.py:304
  (21 shorter events, 0.2 us)
Async XLA Ops:
  0.9 32.8 %copy-start = (bf16[256,768]{1,0:T(8,128)(2,1)S(1)}, bf16[256,768]{1,0:T(8,128)(2,1)}, u32[]{:S(2)}) copy-start(bf16[256,768]{1,0:T(8,128)(2,1)} %refs_0_.1) | copy-start | bytes 1179652
  0.9 9.7 %collective-permute-start.1 = (bf16[64,768]{1,0:T(8,128)(2,1)S(1)}, bf16[64,768]{1,0:T(8,128)(2,1)S(1)}, u32[]{:S(2)}, u32[]{:S(2)}) collective-permute-start(bf16[64,768]{1,0:T(8,128)(2,1)S(1)} %constant_dynamic-slice_fusion.23), channel_id=1, source_target_pairs={{0,24},{4,28},{8,16},{12,20},{16,8},{20,12},{24,0},{28,4},{1,25},{... | collective-permute-start | bytes 294920 | tf_op jit(solution)/shard_map/ppermute | solution.py:362
  6.1 8.4 %collective-permute-start = (bf16[64,768]{1,0:T(8,128)(2,1)S(1)}, bf16[64,768]{1,0:T(8,128)(2,1)S(1)}, u32[]{:S(2)}, u32[]{:S(2)}) collective-permute-start(bf16[64,768]{1,0:T(8,128)(2,1)S(1)} %constant_dynamic-slice_fusion.23), channel_id=1, source_target_pairs={{0,16},{4,20},{8,24},{12,28},{16,0},{20,4},{24,8},{28,12},{1,17},{... | collective-permute-start | bytes 294920 | tf_op jit(solution)/shard_map/ppermute | solution.py:362
  7.0 2.4 %copy-start.1 = (s32[256]{0:T(256)S(1)}, s32[256]{0:T(256)}, u32[]{:S(2)}) copy-start(s32[256]{0:T(256)} %param.3) | copy-start | bytes 3076
  7.0 9.8 %collective-permute-start.2 = (bf16[128,768]{1,0:T(8,128)(2,1)S(1)}, bf16[128,768]{1,0:T(8,128)(2,1)S(1)}, u32[]{:S(2)}, u32[]{:S(2)}) collective-permute-start(bf16[128,768]{1,0:T(8,128)(2,1)S(1)} %constant_dynamic-slice_fusion.22), channel_id=1, source_target_pairs={{0,4},{4,0},{8,12},{12,8},{16,20},{20,16},{24,28},{28,24},{1,5},{5... | collective-permute-start | bytes 589832 | tf_op jit(solution)/shard_map/ppermute | solution.py:362
  8.6 11.1 %collective-permute-start.4 = (bf16[128,768]{1,0:T(8,128)(2,1)S(1)}, bf16[128,768]{1,0:T(8,128)(2,1)S(1)}, u32[]{:S(2)}, u32[]{:S(2)}) collective-permute-start(bf16[128,768]{1,0:T(8,128)(2,1)S(1)} %constant_dynamic-slice_fusion.22), channel_id=1, source_target_pairs={{0,8},{4,12},{8,0},{12,4},{16,24},{20,28},{24,16},{28,20},{1,9},{5... | collective-permute-start | bytes 589832 | tf_op jit(solution)/shard_map/ppermute | solution.py:362
  9.4 7.5 %collective-permute-start.3 = (s32[1,256]{1,0:T(1,128)S(1)}, s32[1,256]{1,0:T(1,128)S(1)}, u32[]{:S(2)}, u32[]{:S(2)}) collective-permute-start(s32[1,256]{1,0:T(1,128)S(1)} %bitcast.48), channel_id=1, source_target_pairs={{0,8},{4,12},{8,0},{12,4},{16,24},{20,28},{24,16},{28,20},{1,9},{5... | collective-permute-start | bytes 3080 | tf_op jit(solution)/shard_map/ppermute | solution.py:362
  16.8 8.1 %collective-permute-start.7 = (bf16[128,768]{1,0:T(8,128)(2,1)S(1)}, bf16[128,768]{1,0:T(8,128)(2,1)S(1)}, u32[]{:S(2)}, u32[]{:S(2)}) collective-permute-start(bf16[128,768]{1,0:T(8,128)(2,1)S(1)} %pad_maximum_fusion.refs_4_), channel_id=1, source_target_pairs={{0,4},{4,0},{8,12},{12,8},{16,20},{20,16},{24,28},{28,24},{1,5},{5... | collective-permute-start | bytes 589832 | tf_op jit(solution)/shard_map/ppermute | solution.py:362
  17.5 9.3 %collective-permute-start.6 = (bf16[128,768]{1,0:T(8,128)(2,1)S(1)}, bf16[128,768]{1,0:T(8,128)(2,1)S(1)}, u32[]{:S(2)}, u32[]{:S(2)}) collective-permute-start(bf16[128,768]{1,0:T(8,128)(2,1)S(1)} %pad_maximum_fusion.refs_4_), channel_id=1, source_target_pairs={{0,2},{1,3},{2,0},{3,1},{4,6},{5,7},{6,4},{7,5},{8,10},{9,11},{10,... | collective-permute-start | bytes 589832 | tf_op jit(solution)/shard_map/ppermute | solution.py:362
  19.0 4.5 %collective-permute-start.16 = (s32[2,256]{1,0:T(2,128)S(1)}, s32[2,256]{1,0:T(2,128)S(1)}, u32[]{:S(2)}, u32[]{:S(2)}) collective-permute-start(s32[2,256]{1,0:T(2,128)S(1)} %pad_add_fusion.1), channel_id=1, source_target_pairs={{0,16},{4,20},{8,24},{12,28},{16,0},{20,4},{24,8},{28,12},{1,17},{... | collective-permute-start | bytes 6152 | tf_op jit(solution)/shard_map/ppermute | solution.py:362
  19.7 7.1 %collective-permute-start.5 = (bf16[128,768]{1,0:T(8,128)(2,1)S(1)}, bf16[128,768]{1,0:T(8,128)(2,1)S(1)}, u32[]{:S(2)}, u32[]{:S(2)}) collective-permute-start(bf16[128,768]{1,0:T(8,128)(2,1)S(1)} %collective-permute-done.4.refs_2_), channel_id=1, source_target_pairs={{0,4},{4,0},{8,12},{12,8},{16,20},{20,16},{24,28},{28,24},{1,5},{5... | collective-permute-start | bytes 589832 | tf_op jit(solution)/shard_map/ppermute | solution.py:362
  23.5 7.6 %collective-permute-start.17 = (s32[4,256]{1,0:T(4,128)S(1)}, s32[4,256]{1,0:T(4,128)S(1)}, u32[]{:S(2)}, u32[]{:S(2)}) collective-permute-start(s32[4,256]{1,0:T(4,128)S(1)} %pad_add_fusion), channel_id=1, source_target_pairs={{0,4},{4,0},{8,12},{12,8},{16,20},{20,16},{24,28},{28,24},{1,5},{5... | collective-permute-start | bytes 12296 | tf_op jit(solution)/shard_map/ppermute | solution.py:362
  24.9 5.7 %collective-permute-start.8 = (bf16[128,768]{1,0:T(8,128)(2,1)S(1)}, bf16[128,768]{1,0:T(8,128)(2,1)S(1)}, u32[]{:S(2)}, u32[]{:S(2)}) collective-permute-start(bf16[128,768]{1,0:T(8,128)(2,1)S(1)} %collective-permute-done.7.refs_6_), channel_id=1, source_target_pairs={{0,2},{1,3},{2,0},{3,1},{4,6},{5,7},{6,4},{7,5},{8,10},{9,11},{10,... | collective-permute-start | bytes 589832 | tf_op jit(solution)/shard_map/ppermute | solution.py:362
  30.6 1.4 %collective-permute-start.9 = (bf16[128,768]{1,0:T(8,128)(2,1)S(1)}, bf16[128,768]{1,0:T(8,128)(2,1)S(1)}, u32[]{:S(2)}, u32[]{:S(2)}) collective-permute-start(bf16[128,768]{1,0:T(8,128)(2,1)S(1)} %collective-permute-done.2.refs_1_), channel_id=1, source_target_pairs={{0,1},{1,0},{2,3},{3,2},{4,5},{5,4},{6,7},{7,6},{8,9},{9,8},{10,11... | collective-permute-start | bytes 589832 | tf_op jit(solution)/shard_map/ppermute | solution.py:362
  30.6 1.7 %collective-permute-start.10 = (bf16[128,768]{1,0:T(8,128)(2,1)S(1)}, bf16[128,768]{1,0:T(8,128)(2,1)S(1)}, u32[]{:S(2)}, u32[]{:S(2)}) collective-permute-start(bf16[128,768]{1,0:T(8,128)(2,1)S(1)} %collective-permute-done.4.refs_2_), channel_id=1, source_target_pairs={{0,1},{1,0},{2,3},{3,2},{4,5},{5,4},{6,7},{7,6},{8,9},{9,8},{10,11... | collective-permute-start | bytes 589832 | tf_op jit(solution)/shard_map/ppermute | solution.py:362
  31.1 1.6 %collective-permute-start.11 = (bf16[128,768]{1,0:T(8,128)(2,1)S(1)}, bf16[128,768]{1,0:T(8,128)(2,1)S(1)}, u32[]{:S(2)}, u32[]{:S(2)}) collective-permute-start(bf16[128,768]{1,0:T(8,128)(2,1)S(1)} %collective-permute-done.5.refs_3_), channel_id=1, source_target_pairs={{0,1},{1,0},{2,3},{3,2},{4,5},{5,4},{6,7},{7,6},{8,9},{9,8},{10,11... | collective-permute-start | bytes 589832 | tf_op jit(solution)/shard_map/ppermute | solution.py:362
  31.2 1.7 %collective-permute-start.12 = (bf16[128,768]{1,0:T(8,128)(2,1)S(1)}, bf16[128,768]{1,0:T(8,128)(2,1)S(1)}, u32[]{:S(2)}, u32[]{:S(2)}) collective-permute-start(bf16[128,768]{1,0:T(8,128)(2,1)S(1)} %pad_maximum_fusion.refs_4_), channel_id=1, source_target_pairs={{0,1},{1,0},{2,3},{3,2},{4,5},{5,4},{6,7},{7,6},{8,9},{9,8},{10,11... | collective-permute-start | bytes 589832 | tf_op jit(solution)/shard_map/ppermute | solution.py:362
  31.7 1.5 %collective-permute-start.13 = (bf16[128,768]{1,0:T(8,128)(2,1)S(1)}, bf16[128,768]{1,0:T(8,128)(2,1)S(1)}, u32[]{:S(2)}, u32[]{:S(2)}) collective-permute-start(bf16[128,768]{1,0:T(8,128)(2,1)S(1)} %collective-permute-done.6.refs_5_), channel_id=1, source_target_pairs={{0,1},{1,0},{2,3},{3,2},{4,5},{5,4},{6,7},{7,6},{8,9},{9,8},{10,11... | collective-permute-start | bytes 589832 | tf_op jit(solution)/shard_map/ppermute | solution.py:362
  32.0 1.4 %collective-permute-start.14 = (bf16[128,768]{1,0:T(8,128)(2,1)S(1)}, bf16[128,768]{1,0:T(8,128)(2,1)S(1)}, u32[]{:S(2)}, u32[]{:S(2)}) collective-permute-start(bf16[128,768]{1,0:T(8,128)(2,1)S(1)} %collective-permute-done.7.refs_6_), channel_id=1, source_target_pairs={{0,1},{1,0},{2,3},{3,2},{4,5},{5,4},{6,7},{7,6},{8,9},{9,8},{10,11... | collective-permute-start | bytes 589832 | tf_op jit(solution)/shard_map/ppermute | solution.py:362
  32.3 1.4 %collective-permute-start.15 = (bf16[128,768]{1,0:T(8,128)(2,1)S(1)}, bf16[128,768]{1,0:T(8,128)(2,1)S(1)}, u32[]{:S(2)}, u32[]{:S(2)}) collective-permute-start(bf16[128,768]{1,0:T(8,128)(2,1)S(1)} %collective-permute-done.8.refs_7_), channel_id=1, source_target_pairs={{0,1},{1,0},{2,3},{3,2},{4,5},{5,4},{6,7},{7,6},{8,9},{9,8},{10,11... | collective-permute-start | bytes 589832 | tf_op jit(solution)/shard_map/ppermute | solution.py:362
where the time goes:
time: 60.6 us; the launch traced here: 60.5 us
  Pallas kernels  26.7 us (44%)
  starting transfers between devices  16.9 us (28%)
  waiting for transfers between devices  14.7 us (24%)
  local copies, waits for them, and re-layouts  2.14 us (4%)
    pallas_call x1, Pallas kernels, scores_of(): pl.pallas_call(functools.partial(score_kernel, sizes), out_shape=jax.Shap...  26.7 us
    ppermute x18, starting transfers between devices, exchange(): lax.ppermute(value, axis, [(i, i ^ flip) for i in range(lax.axis_size(axi...  16.9 us
    ppermute x18, waiting for transfers between devices, exchange(): lax.ppermute(value, axis, [(i, i ^ flip) for i in range(lax.axis_size(axi...  14.7 us
  transfers between devices with their start and end apart: 18, of which 11 were waited for; matrix products, arithmetic and copies ran while one was open for 2% of the time, Pallas kernels for 0%

commit v1 on v0

--- a/solution.py
+++ b/solution.py
@@ -24,7 +24,7 @@
     lane = lax.broadcasted_iota(jnp.int32, shape, 1)
     sub = lax.broadcasted_iota(jnp.int32, shape, 0)
     count = BLK // SUB
-    slots = count * SUB // 2
+    slots = (count - 1) * SUB // 2
     jobs = list(jobs)
     total = len(jobs)
     rows = [block[SUB * i : SUB * (i + 1), :] for i in range(count)]
@@ -375,24 +375,22 @@
     zone = exchange(own_half, "dp", 2)
     near = exchange(own_half, "dp", 1)
     ids = cluster_ids[None]
-    next_ids = exchange(ids, "dp", 2)
+    next_ids = exchange(ids, "dp", 1)
     far, near, next_ids = lax.optimization_barrier((far, near, next_ids))
 
     far_near = exchange(far, "dp", 1)
     far_side = exchange(far, "mp", 2)
     zone_near = exchange(zone, "dp", 1)
     ids = jnp.concatenate([ids, next_ids], axis=0)
+    ids = jnp.concatenate([ids, exchange(ids, "dp", 2)], axis=0)
+    far_near_side = exchange(far_near, "mp", 2)
+
     ids = jnp.concatenate([ids, exchange(ids, "dp", 4)], axis=0)
-    far_near_side = exchange(far_near, "mp", 2)
-
-    ids = jnp.concatenate([ids, exchange(ids, "dp", 1)], axis=0)
-    place = {0: 0, 2: 1, 4: 2, 6: 3, 1: 4, 3: 5, 5: 6, 7: 7}
-
     held = lax.optimization_barrier([near, zone, zone_near, far, far_side, far_near, far_near_side])
     pieces = [embeddings] + held + [exchange(value, "mp", 1) for value in held]
 
     def ids_of(sources, start, size):
-        return [lax.dynamic_slice_in_dim(ids[place[n]], start, size, 0) for n in sources]
+        return [lax.dynamic_slice_in_dim(ids[n], start, size, 0) for n in sources]
 
     orders = [cluster_ids]
     for c in (core, 1 - core):

time: 60.6 us -> 58.3 us (0.962)
  waiting for transfers between devices: 14.7 us -> 13.6 us
  starting transfers between devices: 16.9 us -> 15.8 us
    ppermute x18, starting transfers between devices: 16.9 us -> 15.8 us  [exchange(): lax.ppermute(value, axis, [(i, i ^ flip) for i in range(lax.axis_size(axi...]
    ppermute x18, waiting for transfers between devices: 14.7 us -> 13.6 us  [exchange(): lax.ppermute(value, axis, [(i, i ^ flip) for i in range(lax.axis_size(axi...]
  transfers between devices with their start and end apart: 18 -> 18, of which waited for: 11 -> 10; matrix products, arithmetic and copies ran while one was open for 2% -> 2% of each run, Pallas kernels for 0% -> 0%
where the time goes in v1:
time: 58.3 us; the launch traced here: 58.1 us
  Pallas kernels  26.5 us (45%)
  starting transfers between devices  15.8 us (27%)
  waiting for transfers between devices  13.6 us (23%)
  local copies, waits for them, and re-layouts  2.15 us (4%)
    pallas_call x1, Pallas kernels, scores_of(): pl.pallas_call(functools.partial(score_kernel, sizes), out_shape=jax.Shap...  26.5 us
    ppermute x18, starting transfers between devices, exchange(): lax.ppermute(value, axis, [(i, i ^ flip) for i in range(lax.axis_size(axi...  15.8 us
    ppermute x18, waiting for transfers between devices, exchange(): lax.ppermute(value, axis, [(i, i ^ flip) for i in range(lax.axis_size(axi...  13.6 us
  transfers between devices with their start and end apart: 18, of which 10 were waited for; matrix products, arithmetic and copies ran while one was open for 2% of the time, Pallas kernels for 0%

profile of v1, /device:TPU:0, one launch (start us, length us, event | category | flops | bytes accessed | tf_op | source)
XLA Modules:
  0.0 58.1 jit_solution(10478455979203891168)
XLA Ops:
  0.0 0.9 %constant_dynamic-slice_fusion.23 = bf16[64,768]{1,0:T(8,128)(2,1)S(1)} fusion(bf16[256,768]{1,0:T(8,128)(2,1)} %refs_0_.1, s32[]{:T(128)S(6)} %dynamic_slice.119), kind=kLoop, calls=%fused_computation.24 | loop fusion | bytes 196612 | tf_op jit(solution)/shard_map/dynamic_slice | solution.py:373
  0.9 0.0 copy-start
  0.9 5.1 %collective-permute-start.1 = (bf16[64,768]{1,0:T(8,128)(2,1)S(1)}, bf16[64,768]{1,0:T(8,128)(2,1)S(1)}, u32[]{:S(2)}, u32[]{:S(2)}) collective-permute-start(bf16[64,768]{1,0:T(8,128)(2,1)S(1)} %constant_dynamic-slice_fusion.23), channel_id=1, source_target_pairs={{0,24},{4,28},{8,16},{12,20},{16,8},{20,12},{24,0},{28,4},{1,25},{... | collective-permute-start | bytes 294920 | tf_op jit(solution)/shard_map/ppermute | solution.py:362
  6.1 0.9 %constant_dynamic-slice_fusion.22 = bf16[128,768]{1,0:T(8,128)(2,1)S(1)} fusion(bf16[256,768]{1,0:T(8,128)(2,1)} %refs_0_.1, s32[]{:T(128)S(6)} %select_n.57), kind=kLoop, calls=%fused_computation.23 | loop fusion | bytes 393220 | tf_op jit(solution)/shard_map/dynamic_slice | solution.py:372
  7.0 1.6 %collective-permute-start.2 = (bf16[128,768]{1,0:T(8,128)(2,1)S(1)}, bf16[128,768]{1,0:T(8,128)(2,1)S(1)}, u32[]{:S(2)}, u32[]{:S(2)}) collective-permute-start(bf16[128,768]{1,0:T(8,128)(2,1)S(1)} %constant_dynamic-slice_fusion.22), channel_id=1, source_target_pairs={{0,4},{4,0},{8,12},{12,8},{16,20},{20,16},{24,28},{28,24},{1,5},{5... | collective-permute-start | bytes 589832 | tf_op jit(solution)/shard_map/ppermute | solution.py:362
  8.6 0.8 %collective-permute-start.4 = (bf16[128,768]{1,0:T(8,128)(2,1)S(1)}, bf16[128,768]{1,0:T(8,128)(2,1)S(1)}, u32[]{:S(2)}, u32[]{:S(2)}) collective-permute-start(bf16[128,768]{1,0:T(8,128)(2,1)S(1)} %constant_dynamic-slice_fusion.22), channel_id=1, source_target_pairs={{0,8},{4,12},{8,0},{12,4},{16,24},{20,28},{24,16},{28,20},{1,9},{5... | collective-permute-start | bytes 589832 | tf_op jit(solution)/shard_map/ppermute | solution.py:362
  9.4 0.4 collective-permute-start.3
  9.7 4.7 %collective-permute-done = bf16[64,768]{1,0:T(8,128)(2,1)S(1)} collective-permute-done((bf16[64,768]{1,0:T(8,128)(2,1)S(1)}, bf16[64,768]{1,0:T(8,128)(2,1)S(1)}, u32[]{:S(2)}, u32[]{:S(2)}) %collective-permute-start) | collective-permute-done | bytes 98336 | tf_op jit(solution)/shard_map/ppermute | solution.py:362
  14.5 1.6 %collective-permute-start.7 = (bf16[128,768]{1,0:T(8,128)(2,1)S(1)}, bf16[128,768]{1,0:T(8,128)(2,1)S(1)}, u32[]{:S(2)}, u32[]{:S(2)}) collective-permute-start(bf16[128,768]{1,0:T(8,128)(2,1)S(1)} %pad_maximum_fusion.refs_4_), channel_id=1, source_target_pairs={{0,4},{4,0},{8,12},{12,8},{16,20},{20,16},{24,28},{28,24},{1,5},{5... | collective-permute-start | bytes 589832 | tf_op jit(solution)/shard_map/ppermute | solution.py:362
  16.0 1.5 %collective-permute-start.6 = (bf16[128,768]{1,0:T(8,128)(2,1)S(1)}, bf16[128,768]{1,0:T(8,128)(2,1)S(1)}, u32[]{:S(2)}, u32[]{:S(2)}) collective-permute-start(bf16[128,768]{1,0:T(8,128)(2,1)S(1)} %pad_maximum_fusion.refs_4_), channel_id=1, source_target_pairs={{0,2},{1,3},{2,0},{3,1},{4,6},{5,7},{6,4},{7,5},{8,10},{9,11},{10,... | collective-permute-start | bytes 589832 | tf_op jit(solution)/shard_map/ppermute | solution.py:362
  17.6 0.6 collective-permute-start.5
  18.2 3.0 %collective-permute-done.16 = s32[2,256]{1,0:T(2,128)S(1)} collective-permute-done((s32[2,256]{1,0:T(2,128)S(1)}, s32[2,256]{1,0:T(2,128)S(1)}, u32[]{:S(2)}, u32[]{:S(2)}) %collective-permute-start.16) | collective-permute-done | bytes 2080 | tf_op jit(solution)/shard_map/ppermute | solution.py:362
  21.1 1.7 %collective-permute-start.17 = (s32[4,256]{1,0:T(4,128)S(1)}, s32[4,256]{1,0:T(4,128)S(1)}, u32[]{:S(2)}, u32[]{:S(2)}) collective-permute-start(s32[4,256]{1,0:T(4,128)S(1)} %pad_add_fusion), channel_id=1, source_target_pairs={{0,16},{4,20},{8,24},{12,28},{16,0},{20,4},{24,8},{28,12},{1,17},{... | collective-permute-start | bytes 12296 | tf_op jit(solution)/shard_map/ppermute | solution.py:362
  22.8 1.0 %collective-permute-start.8 = (bf16[128,768]{1,0:T(8,128)(2,1)S(1)}, bf16[128,768]{1,0:T(8,128)(2,1)S(1)}, u32[]{:S(2)}, u32[]{:S(2)}) collective-permute-start(bf16[128,768]{1,0:T(8,128)(2,1)S(1)} %collective-permute-done.7.refs_6_), channel_id=1, source_target_pairs={{0,2},{1,3},{2,0},{3,1},{4,6},{5,7},{6,4},{7,5},{8,10},{9,11},{10,... | collective-permute-start | bytes 589832 | tf_op jit(solution)/shard_map/ppermute | solution.py:362
  23.9 0.7 %collective-permute-done.5.refs_3_ = bf16[128,768]{1,0:T(8,128)(2,1)S(1)} collective-permute-done((bf16[128,768]{1,0:T(8,128)(2,1)S(1)}, bf16[128,768]{1,0:T(8,128)(2,1)S(1)}, u32[]{:S(2)}, u32[]{:S(2)}) %collective-permute-start.5) | collective-permute-done | bytes 196640 | tf_op jit(solution)/shard_map/ppermute | solution.py:362
  24.6 3.9 %collective-permute-done.8.refs_7_ = bf16[128,768]{1,0:T(8,128)(2,1)S(1)} collective-permute-done((bf16[128,768]{1,0:T(8,128)(2,1)S(1)}, bf16[128,768]{1,0:T(8,128)(2,1)S(1)}, u32[]{:S(2)}, u32[]{:S(2)}) %collective-permute-start.8) | collective-permute-done | bytes 196640 | tf_op jit(solution)/shard_map/ppermute | solution.py:362
  28.5 0.5 collective-permute-start.10
  29.0 0.1 collective-permute-start.11
  29.1 0.5 collective-permute-start.12
  29.6 0.1 collective-permute-start.13
  29.7 0.3 collective-permute-done.9.refs_8_
  29.9 0.2 collective-permute-start.14
  30.1 0.1 collective-permute-done.10.refs_9_
  30.2 0.2 collective-permute-start.15
  30.4 0.1 fusion.20
  30.5 0.1 fusion.16
  30.6 0.1 concatenate.16
  30.7 0.1 collective-permute-done.12.refs_11_
  30.8 0.3 collective-permute-done.13.refs_12_
  31.1 0.3 collective-permute-done.14.refs_13_
  31.4 0.3 collective-permute-done.15.refs_14_
  31.7 26.5 %shard_map.28 = f32[1,256]{1,0:T(1,128)} custom-call(bf16[256,768]{1,0:T(8,128)(2,1)S(1)} %copy-done, bf16[128,768]{1,0:T(8,128)(2,1)S(1)} %collective-permute-done.2.refs_1_, bf16[128,768]{1,0:T(8,128)(2,1)S(1)} %collective-permute-done.4.refs_2_, bf16[128,768]{1,0:T(8,128)(2,1)S(1)} %collective-permute-done.5.refs_3_, ...), custom_call_target="tpu_custom_call" | custom-call | tf_op jit(solution)/shard_map/pallas_call | solution.py:304
  (21 shorter events, 0.1 us)
Async XLA Ops:
  0.9 30.7 %copy-start = (bf16[256,768]{1,0:T(8,128)(2,1)S(1)}, bf16[256,768]{1,0:T(8,128)(2,1)}, u32[]{:S(2)}) copy-start(bf16[256,768]{1,0:T(8,128)(2,1)} %refs_0_.1) | copy-start | bytes 1179652
  0.9 8.8 %collective-permute-start.1 = (bf16[64,768]{1,0:T(8,128)(2,1)S(1)}, bf16[64,768]{1,0:T(8,128)(2,1)S(1)}, u32[]{:S(2)}, u32[]{:S(2)}) collective-permute-start(bf16[64,768]{1,0:T(8,128)(2,1)S(1)} %constant_dynamic-slice_fusion.23), channel_id=1, source_target_pairs={{0,24},{4,28},{8,16},{12,20},{16,8},{20,12},{24,0},{28,4},{1,25},{... | collective-permute-start | bytes 294920 | tf_op jit(solution)/shard_map/ppermute | solution.py:362
  6.1 8.4 %collective-permute-start = (bf16[64,768]{1,0:T(8,128)(2,1)S(1)}, bf16[64,768]{1,0:T(8,128)(2,1)S(1)}, u32[]{:S(2)}, u32[]{:S(2)}) collective-permute-start(bf16[64,768]{1,0:T(8,128)(2,1)S(1)} %constant_dynamic-slice_fusion.23), channel_id=1, source_target_pairs={{0,16},{4,20},{8,24},{12,28},{16,0},{20,4},{24,8},{28,12},{1,17},{... | collective-permute-start | bytes 294920 | tf_op jit(solution)/shard_map/ppermute | solution.py:362
  7.0 2.4 %copy-start.1 = (s32[256]{0:T(256)S(1)}, s32[256]{0:T(256)}, u32[]{:S(2)}) copy-start(s32[256]{0:T(256)} %param.3) | copy-start | bytes 3076
  7.0 7.4 %collective-permute-start.2 = (bf16[128,768]{1,0:T(8,128)(2,1)S(1)}, bf16[128,768]{1,0:T(8,128)(2,1)S(1)}, u32[]{:S(2)}, u32[]{:S(2)}) collective-permute-start(bf16[128,768]{1,0:T(8,128)(2,1)S(1)} %constant_dynamic-slice_fusion.22), channel_id=1, source_target_pairs={{0,4},{4,0},{8,12},{12,8},{16,20},{20,16},{24,28},{28,24},{1,5},{5... | collective-permute-start | bytes 589832 | tf_op jit(solution)/shard_map/ppermute | solution.py:362
  8.6 9.0 %collective-permute-start.4 = (bf16[128,768]{1,0:T(8,128)(2,1)S(1)}, bf16[128,768]{1,0:T(8,128)(2,1)S(1)}, u32[]{:S(2)}, u32[]{:S(2)}) collective-permute-start(bf16[128,768]{1,0:T(8,128)(2,1)S(1)} %constant_dynamic-slice_fusion.22), channel_id=1, source_target_pairs={{0,8},{4,12},{8,0},{12,4},{16,24},{20,28},{24,16},{28,20},{1,9},{5... | collective-permute-start | bytes 589832 | tf_op jit(solution)/shard_map/ppermute | solution.py:362
  9.4 5.1 %collective-permute-start.3 = (s32[1,256]{1,0:T(1,128)S(1)}, s32[1,256]{1,0:T(1,128)S(1)}, u32[]{:S(2)}, u32[]{:S(2)}) collective-permute-start(s32[1,256]{1,0:T(1,128)S(1)} %bitcast.48), channel_id=1, source_target_pairs={{0,4},{4,0},{8,12},{12,8},{16,20},{20,16},{24,28},{28,24},{1,5},{5... | collective-permute-start | bytes 3080 | tf_op jit(solution)/shard_map/ppermute | solution.py:362
  14.5 8.4 %collective-permute-start.7 = (bf16[128,768]{1,0:T(8,128)(2,1)S(1)}, bf16[128,768]{1,0:T(8,128)(2,1)S(1)}, u32[]{:S(2)}, u32[]{:S(2)}) collective-permute-start(bf16[128,768]{1,0:T(8,128)(2,1)S(1)} %pad_maximum_fusion.refs_4_), channel_id=1, source_target_pairs={{0,4},{4,0},{8,12},{12,8},{16,20},{20,16},{24,28},{28,24},{1,5},{5... | collective-permute-start | bytes 589832 | tf_op jit(solution)/shard_map/ppermute | solution.py:362
  16.0 8.5 %collective-permute-start.6 = (bf16[128,768]{1,0:T(8,128)(2,1)S(1)}, bf16[128,768]{1,0:T(8,128)(2,1)S(1)}, u32[]{:S(2)}, u32[]{:S(2)}) collective-permute-start(bf16[128,768]{1,0:T(8,128)(2,1)S(1)} %pad_maximum_fusion.refs_4_), channel_id=1, source_target_pairs={{0,2},{1,3},{2,0},{3,1},{4,6},{5,7},{6,4},{7,5},{8,10},{9,11},{10,... | collective-permute-start | bytes 589832 | tf_op jit(solution)/shard_map/ppermute | solution.py:362
  17.5 3.6 %collective-permute-start.16 = (s32[2,256]{1,0:T(2,128)S(1)}, s32[2,256]{1,0:T(2,128)S(1)}, u32[]{:S(2)}, u32[]{:S(2)}) collective-permute-start(s32[2,256]{1,0:T(2,128)S(1)} %pad_add_fusion.1), channel_id=1, source_target_pairs={{0,8},{4,12},{8,0},{12,4},{16,24},{20,28},{24,16},{28,20},{1,9},{5... | collective-permute-start | bytes 6152 | tf_op jit(solution)/shard_map/ppermute | solution.py:362
  17.6 7.0 %collective-permute-start.5 = (bf16[128,768]{1,0:T(8,128)(2,1)S(1)}, bf16[128,768]{1,0:T(8,128)(2,1)S(1)}, u32[]{:S(2)}, u32[]{:S(2)}) collective-permute-start(bf16[128,768]{1,0:T(8,128)(2,1)S(1)} %collective-permute-done.4.refs_2_), channel_id=1, source_target_pairs={{0,4},{4,0},{8,12},{12,8},{16,20},{20,16},{24,28},{28,24},{1,5},{5... | collective-permute-start | bytes 589832 | tf_op jit(solution)/shard_map/ppermute | solution.py:362
  21.1 7.9 %collective-permute-start.17 = (s32[4,256]{1,0:T(4,128)S(1)}, s32[4,256]{1,0:T(4,128)S(1)}, u32[]{:S(2)}, u32[]{:S(2)}) collective-permute-start(s32[4,256]{1,0:T(4,128)S(1)} %pad_add_fusion), channel_id=1, source_target_pairs={{0,16},{4,20},{8,24},{12,28},{16,0},{20,4},{24,8},{28,12},{1,17},{... | collective-permute-start | bytes 12296 | tf_op jit(solution)/shard_map/ppermute | solution.py:362
  22.8 5.7 %collective-permute-start.8 = (bf16[128,768]{1,0:T(8,128)(2,1)S(1)}, bf16[128,768]{1,0:T(8,128)(2,1)S(1)}, u32[]{:S(2)}, u32[]{:S(2)}) collective-permute-start(bf16[128,768]{1,0:T(8,128)(2,1)S(1)} %collective-permute-done.7.refs_6_), channel_id=1, source_target_pairs={{0,2},{1,3},{2,0},{3,1},{4,6},{5,7},{6,4},{7,5},{8,10},{9,11},{10,... | collective-permute-start | bytes 589832 | tf_op jit(solution)/shard_map/ppermute | solution.py:362
  28.5 1.4 %collective-permute-start.9 = (bf16[128,768]{1,0:T(8,128)(2,1)S(1)}, bf16[128,768]{1,0:T(8,128)(2,1)S(1)}, u32[]{:S(2)}, u32[]{:S(2)}) collective-permute-start(bf16[128,768]{1,0:T(8,128)(2,1)S(1)} %collective-permute-done.2.refs_1_), channel_id=1, source_target_pairs={{0,1},{1,0},{2,3},{3,2},{4,5},{5,4},{6,7},{7,6},{8,9},{9,8},{10,11... | collective-permute-start | bytes 589832 | tf_op jit(solution)/shard_map/ppermute | solution.py:362
  28.5 1.7 %collective-permute-start.10 = (bf16[128,768]{1,0:T(8,128)(2,1)S(1)}, bf16[128,768]{1,0:T(8,128)(2,1)S(1)}, u32[]{:S(2)}, u32[]{:S(2)}) collective-permute-start(bf16[128,768]{1,0:T(8,128)(2,1)S(1)} %collective-permute-done.4.refs_2_), channel_id=1, source_target_pairs={{0,1},{1,0},{2,3},{3,2},{4,5},{5,4},{6,7},{7,6},{8,9},{9,8},{10,11... | collective-permute-start | bytes 589832 | tf_op jit(solution)/shard_map/ppermute | solution.py:362
  29.0 1.7 %collective-permute-start.11 = (bf16[128,768]{1,0:T(8,128)(2,1)S(1)}, bf16[128,768]{1,0:T(8,128)(2,1)S(1)}, u32[]{:S(2)}, u32[]{:S(2)}) collective-permute-start(bf16[128,768]{1,0:T(8,128)(2,1)S(1)} %collective-permute-done.5.refs_3_), channel_id=1, source_target_pairs={{0,1},{1,0},{2,3},{3,2},{4,5},{5,4},{6,7},{7,6},{8,9},{9,8},{10,11... | collective-permute-start | bytes 589832 | tf_op jit(solution)/shard_map/ppermute | solution.py:362
  29.1 1.7 %collective-permute-start.12 = (bf16[128,768]{1,0:T(8,128)(2,1)S(1)}, bf16[128,768]{1,0:T(8,128)(2,1)S(1)}, u32[]{:S(2)}, u32[]{:S(2)}) collective-permute-start(bf16[128,768]{1,0:T(8,128)(2,1)S(1)} %pad_maximum_fusion.refs_4_), channel_id=1, source_target_pairs={{0,1},{1,0},{2,3},{3,2},{4,5},{5,4},{6,7},{7,6},{8,9},{9,8},{10,11... | collective-permute-start | bytes 589832 | tf_op jit(solution)/shard_map/ppermute | solution.py:362
  29.6 1.5 %collective-permute-start.13 = (bf16[128,768]{1,0:T(8,128)(2,1)S(1)}, bf16[128,768]{1,0:T(8,128)(2,1)S(1)}, u32[]{:S(2)}, u32[]{:S(2)}) collective-permute-start(bf16[128,768]{1,0:T(8,128)(2,1)S(1)} %collective-permute-done.6.refs_5_), channel_id=1, source_target_pairs={{0,1},{1,0},{2,3},{3,2},{4,5},{5,4},{6,7},{7,6},{8,9},{9,8},{10,11... | collective-permute-start | bytes 589832 | tf_op jit(solution)/shard_map/ppermute | solution.py:362
  29.9 1.4 %collective-permute-start.14 = (bf16[128,768]{1,0:T(8,128)(2,1)S(1)}, bf16[128,768]{1,0:T(8,128)(2,1)S(1)}, u32[]{:S(2)}, u32[]{:S(2)}) collective-permute-start(bf16[128,768]{1,0:T(8,128)(2,1)S(1)} %collective-permute-done.7.refs_6_), channel_id=1, source_target_pairs={{0,1},{1,0},{2,3},{3,2},{4,5},{5,4},{6,7},{7,6},{8,9},{9,8},{10,11... | collective-permute-start | bytes 589832 | tf_op jit(solution)/shard_map/ppermute | solution.py:362
  30.2 1.4 %collective-permute-start.15 = (bf16[128,768]{1,0:T(8,128)(2,1)S(1)}, bf16[128,768]{1,0:T(8,128)(2,1)S(1)}, u32[]{:S(2)}, u32[]{:S(2)}) collective-permute-start(bf16[128,768]{1,0:T(8,128)(2,1)S(1)} %collective-permute-done.8.refs_7_), channel_id=1, source_target_pairs={{0,1},{1,0},{2,3},{3,2},{4,5},{5,4},{6,7},{7,6},{8,9},{9,8},{10,11... | collective-permute-start | bytes 589832 | tf_op jit(solution)/shard_map/ppermute | solution.py:362

commit v2 on v1

--- a/solution.py
+++ b/solution.py
@@ -382,10 +382,10 @@
     far_side = exchange(far, "mp", 2)
     zone_near = exchange(zone, "dp", 1)
     ids = jnp.concatenate([ids, next_ids], axis=0)
-    ids = jnp.concatenate([ids, exchange(ids, "dp", 2)], axis=0)
+    far_near, ids = lax.optimization_barrier((far_near, ids))
     far_near_side = exchange(far_near, "mp", 2)
-
-    ids = jnp.concatenate([ids, exchange(ids, "dp", 4)], axis=0)
+    for flip in (2, 4):
+        ids = jnp.concatenate([ids, exchange(ids, "dp", flip)], axis=0)
     held = lax.optimization_barrier([near, zone, zone_near, far, far_side, far_near, far_near_side])
     pieces = [embeddings] + held + [exchange(value, "mp", 1) for value in held]
 

time: 58.3 us -> 59.5 us (1.021)
  waiting for transfers between devices: 13.6 us -> 14.3 us
    ppermute x18, waiting for transfers between devices: 13.6 us -> 14.3 us  [exchange(): lax.ppermute(value, axis, [(i, i ^ flip) for i in range(lax.axis_size(axi...]
where the time goes in v2:
time: 59.5 us; the launch traced here: 59.3 us
  Pallas kernels  26.5 us (45%)
  starting transfers between devices  16.3 us (27%)
  waiting for transfers between devices  14.3 us (24%)
  local copies, waits for them, and re-layouts  2.15 us (4%)
    pallas_call x1, Pallas kernels, scores_of(): pl.pallas_call(functools.partial(score_kernel, sizes), out_shape=jax.Shap...  26.5 us
    ppermute x18, starting transfers between devices, exchange(): lax.ppermute(value, axis, [(i, i ^ flip) for i in range(lax.axis_size(axi...  16.3 us
    ppermute x18, waiting for transfers between devices, exchange(): lax.ppermute(value, axis, [(i, i ^ flip) for i in range(lax.axis_size(axi...  14.3 us
  transfers between devices with their start and end apart: 18, of which 10 were waited for; matrix products, arithmetic and copies ran while one was open for 2% of the time, Pallas kernels for 0%

profile of v2, /device:TPU:0, one launch (start us, length us, event | category | flops | bytes accessed | tf_op | source)
XLA Modules:
  0.0 59.3 jit_solution(12152220812506364662)
XLA Ops:
  0.0 0.9 %constant_dynamic-slice_fusion.23 = bf16[64,768]{1,0:T(8,128)(2,1)S(1)} fusion(bf16[256,768]{1,0:T(8,128)(2,1)} %refs_0_.1, s32[]{:T(128)S(6)} %dynamic_slice.119), kind=kLoop, calls=%fused_computation.24 | loop fusion | bytes 196612 | tf_op jit(solution)/shard_map/dynamic_slice | solution.py:373
  0.9 0.0 copy-start
  0.9 5.1 %collective-permute-start.1 = (bf16[64,768]{1,0:T(8,128)(2,1)S(1)}, bf16[64,768]{1,0:T(8,128)(2,1)S(1)}, u32[]{:S(2)}, u32[]{:S(2)}) collective-permute-start(bf16[64,768]{1,0:T(8,128)(2,1)S(1)} %constant_dynamic-slice_fusion.23), channel_id=1, source_target_pairs={{0,24},{4,28},{8,16},{12,20},{16,8},{20,12},{24,0},{28,4},{1,25},{... | collective-permute-start | bytes 294920 | tf_op jit(solution)/shard_map/ppermute | solution.py:362
  6.1 0.9 %constant_dynamic-slice_fusion.22 = bf16[128,768]{1,0:T(8,128)(2,1)S(1)} fusion(bf16[256,768]{1,0:T(8,128)(2,1)} %refs_0_.1, s32[]{:T(128)S(6)} %select_n.57), kind=kLoop, calls=%fused_computation.23 | loop fusion | bytes 393220 | tf_op jit(solution)/shard_map/dynamic_slice | solution.py:372
  7.0 0.0 copy-start.1
  7.0 1.6 %collective-permute-start.2 = (bf16[128,768]{1,0:T(8,128)(2,1)S(1)}, bf16[128,768]{1,0:T(8,128)(2,1)S(1)}, u32[]{:S(2)}, u32[]{:S(2)}) collective-permute-start(bf16[128,768]{1,0:T(8,128)(2,1)S(1)} %constant_dynamic-slice_fusion.22), channel_id=1, source_target_pairs={{0,4},{4,0},{8,12},{12,8},{16,20},{20,16},{24,28},{28,24},{1,5},{5... | collective-permute-start | bytes 589832 | tf_op jit(solution)/shard_map/ppermute | solution.py:362
  8.6 0.8 %collective-permute-start.4 = (bf16[128,768]{1,0:T(8,128)(2,1)S(1)}, bf16[128,768]{1,0:T(8,128)(2,1)S(1)}, u32[]{:S(2)}, u32[]{:S(2)}) collective-permute-start(bf16[128,768]{1,0:T(8,128)(2,1)S(1)} %constant_dynamic-slice_fusion.22), channel_id=1, source_target_pairs={{0,8},{4,12},{8,0},{12,4},{16,24},{20,28},{24,16},{28,20},{1,9},{5... | collective-permute-start | bytes 589832 | tf_op jit(solution)/shard_map/ppermute | solution.py:362
  9.4 0.4 collective-permute-start.3
  9.7 4.7 %collective-permute-done = bf16[64,768]{1,0:T(8,128)(2,1)S(1)} collective-permute-done((bf16[64,768]{1,0:T(8,128)(2,1)S(1)}, bf16[64,768]{1,0:T(8,128)(2,1)S(1)}, u32[]{:S(2)}, u32[]{:S(2)}) %collective-permute-start) | collective-permute-done | bytes 98336 | tf_op jit(solution)/shard_map/ppermute | solution.py:362
  14.5 1.6 %collective-permute-start.7 = (bf16[128,768]{1,0:T(8,128)(2,1)S(1)}, bf16[128,768]{1,0:T(8,128)(2,1)S(1)}, u32[]{:S(2)}, u32[]{:S(2)}) collective-permute-start(bf16[128,768]{1,0:T(8,128)(2,1)S(1)} %pad_maximum_fusion.refs_4_), channel_id=1, source_target_pairs={{0,4},{4,0},{8,12},{12,8},{16,20},{20,16},{24,28},{28,24},{1,5},{5... | collective-permute-start | bytes 589832 | tf_op jit(solution)/shard_map/ppermute | solution.py:362
  16.0 1.5 %collective-permute-start.6 = (bf16[128,768]{1,0:T(8,128)(2,1)S(1)}, bf16[128,768]{1,0:T(8,128)(2,1)S(1)}, u32[]{:S(2)}, u32[]{:S(2)}) collective-permute-start(bf16[128,768]{1,0:T(8,128)(2,1)S(1)} %pad_maximum_fusion.refs_4_), channel_id=1, source_target_pairs={{0,2},{1,3},{2,0},{3,1},{4,6},{5,7},{6,4},{7,5},{8,10},{9,11},{10,... | collective-permute-start | bytes 589832 | tf_op jit(solution)/shard_map/ppermute | solution.py:362
  17.5 0.5 collective-permute-start.5
  18.1 4.1 %collective-permute-done.7.refs_6_ = bf16[128,768]{1,0:T(8,128)(2,1)S(1)} collective-permute-done((bf16[128,768]{1,0:T(8,128)(2,1)S(1)}, bf16[128,768]{1,0:T(8,128)(2,1)S(1)}, u32[]{:S(2)}, u32[]{:S(2)}) %collective-permute-start.7) | collective-permute-done | bytes 196640 | tf_op jit(solution)/shard_map/ppermute | solution.py:362
  22.1 1.7 %collective-permute-start.8 = (bf16[128,768]{1,0:T(8,128)(2,1)S(1)}, bf16[128,768]{1,0:T(8,128)(2,1)S(1)}, u32[]{:S(2)}, u32[]{:S(2)}) collective-permute-start(bf16[128,768]{1,0:T(8,128)(2,1)S(1)} %collective-permute-done.7.refs_6_), channel_id=1, source_target_pairs={{0,2},{1,3},{2,0},{3,1},{4,6},{5,7},{6,4},{7,5},{8,10},{9,11},{10,... | collective-permute-start | bytes 589832 | tf_op jit(solution)/shard_map/ppermute | solution.py:362
  23.9 1.9 %collective-permute-done.16 = s32[2,256]{1,0:T(2,128)S(1)} collective-permute-done((s32[2,256]{1,0:T(2,128)S(1)}, s32[2,256]{1,0:T(2,128)S(1)}, u32[]{:S(2)}, u32[]{:S(2)}) %collective-permute-start.16) | collective-permute-done | bytes 2080 | tf_op jit(solution)/shard_map/ppermute | solution.py:362
  25.7 1.6 %collective-permute-start.17 = (s32[4,256]{1,0:T(4,128)S(1)}, s32[4,256]{1,0:T(4,128)S(1)}, u32[]{:S(2)}, u32[]{:S(2)}) collective-permute-start(s32[4,256]{1,0:T(4,128)S(1)} %pad_add_fusion), channel_id=1, source_target_pairs={{0,16},{4,20},{8,24},{12,28},{16,0},{20,4},{24,8},{28,12},{1,17},{... | collective-permute-start | bytes 12296 | tf_op jit(solution)/shard_map/ppermute | solution.py:362
  27.3 0.5 collective-permute-done.8.refs_7_
  27.8 0.5 collective-permute-start.10
  28.3 1.9 %collective-permute-done.17 = s32[4,256]{1,0:T(4,128)S(1)} collective-permute-done((s32[4,256]{1,0:T(4,128)S(1)}, s32[4,256]{1,0:T(4,128)S(1)}, u32[]{:S(2)}, u32[]{:S(2)}) %collective-permute-start.17) | collective-permute-done | bytes 4128 | tf_op jit(solution)/shard_map/ppermute | solution.py:362
  30.3 0.5 collective-permute-start.12
  30.8 0.1 collective-permute-start.13
  30.8 0.4 collective-permute-start.14
  31.3 0.1 collective-permute-start.15
  31.4 0.1 fusion.20
  31.4 0.1 fusion.16
  31.5 0.1 concatenate.15
  31.6 0.1 collective-permute-done.11.refs_10_
  31.7 0.3 collective-permute-done.12.refs_11_
  32.0 0.3 collective-permute-done.13.refs_12_
  32.3 0.3 collective-permute-done.14.refs_13_
  32.5 0.3 collective-permute-done.15.refs_14_
  32.8 26.5 %shard_map.28 = f32[1,256]{1,0:T(1,128)} custom-call(bf16[256,768]{1,0:T(8,128)(2,1)S(1)} %copy-done, bf16[128,768]{1,0:T(8,128)(2,1)S(1)} %collective-permute-done.2.refs_1_, bf16[128,768]{1,0:T(8,128)(2,1)S(1)} %collective-permute-done.4.refs_2_, bf16[128,768]{1,0:T(8,128)(2,1)S(1)} %collective-permute-done.5.refs_3_, ...), custom_call_target="tpu_custom_call" | custom-call | tf_op jit(solution)/shard_map/pallas_call | solution.py:304
  (22 shorter events, 0.1 us)
Async XLA Ops:
  0.9 31.9 %copy-start = (bf16[256,768]{1,0:T(8,128)(2,1)S(1)}, bf16[256,768]{1,0:T(8,128)(2,1)}, u32[]{:S(2)}) copy-start(bf16[256,768]{1,0:T(8,128)(2,1)} %refs_0_.1) | copy-start | bytes 1179652
  0.9 8.8 %collective-permute-start.1 = (bf16[64,768]{1,0:T(8,128)(2,1)S(1)}, bf16[64,768]{1,0:T(8,128)(2,1)S(1)}, u32[]{:S(2)}, u32[]{:S(2)}) collective-permute-start(bf16[64,768]{1,0:T(8,128)(2,1)S(1)} %constant_dynamic-slice_fusion.23), channel_id=1, source_target_pairs={{0,24},{4,28},{8,16},{12,20},{16,8},{20,12},{24,0},{28,4},{1,25},{... | collective-permute-start | bytes 294920 | tf_op jit(solution)/shard_map/ppermute | solution.py:362
  6.1 8.4 %collective-permute-start = (bf16[64,768]{1,0:T(8,128)(2,1)S(1)}, bf16[64,768]{1,0:T(8,128)(2,1)S(1)}, u32[]{:S(2)}, u32[]{:S(2)}) collective-permute-start(bf16[64,768]{1,0:T(8,128)(2,1)S(1)} %constant_dynamic-slice_fusion.23), channel_id=1, source_target_pairs={{0,16},{4,20},{8,24},{12,28},{16,0},{20,4},{24,8},{28,12},{1,17},{... | collective-permute-start | bytes 294920 | tf_op jit(solution)/shard_map/ppermute | solution.py:362
  7.0 2.4 %copy-start.1 = (s32[256]{0:T(256)S(1)}, s32[256]{0:T(256)}, u32[]{:S(2)}) copy-start(s32[256]{0:T(256)} %param.3) | copy-start | bytes 3076
  7.0 7.4 %collective-permute-start.2 = (bf16[128,768]{1,0:T(8,128)(2,1)S(1)}, bf16[128,768]{1,0:T(8,128)(2,1)S(1)}, u32[]{:S(2)}, u32[]{:S(2)}) collective-permute-start(bf16[128,768]{1,0:T(8,128)(2,1)S(1)} %constant_dynamic-slice_fusion.22), channel_id=1, source_target_pairs={{0,4},{4,0},{8,12},{12,8},{16,20},{20,16},{24,28},{28,24},{1,5},{5... | collective-permute-start | bytes 589832 | tf_op jit(solution)/shard_map/ppermute | solution.py:362
  8.6 8.9 %collective-permute-start.4 = (bf16[128,768]{1,0:T(8,128)(2,1)S(1)}, bf16[128,768]{1,0:T(8,128)(2,1)S(1)}, u32[]{:S(2)}, u32[]{:S(2)}) collective-permute-start(bf16[128,768]{1,0:T(8,128)(2,1)S(1)} %constant_dynamic-slice_fusion.22), channel_id=1, source_target_pairs={{0,8},{4,12},{8,0},{12,4},{16,24},{20,28},{24,16},{28,20},{1,9},{5... | collective-permute-start | bytes 589832 | tf_op jit(solution)/shard_map/ppermute | solution.py:362
  9.4 5.1 %collective-permute-start.3 = (s32[1,256]{1,0:T(1,128)S(1)}, s32[1,256]{1,0:T(1,128)S(1)}, u32[]{:S(2)}, u32[]{:S(2)}) collective-permute-start(s32[1,256]{1,0:T(1,128)S(1)} %bitcast.48), channel_id=1, source_target_pairs={{0,4},{4,0},{8,12},{12,8},{16,20},{20,16},{24,28},{28,24},{1,5},{5... | collective-permute-start | bytes 3080 | tf_op jit(solution)/shard_map/ppermute | solution.py:362
  14.5 7.7 %collective-permute-start.7 = (bf16[128,768]{1,0:T(8,128)(2,1)S(1)}, bf16[128,768]{1,0:T(8,128)(2,1)S(1)}, u32[]{:S(2)}, u32[]{:S(2)}) collective-permute-start(bf16[128,768]{1,0:T(8,128)(2,1)S(1)} %pad_maximum_fusion.refs_4_), channel_id=1, source_target_pairs={{0,4},{4,0},{8,12},{12,8},{16,20},{20,16},{24,28},{28,24},{1,5},{5... | collective-permute-start | bytes 589832 | tf_op jit(solution)/shard_map/ppermute | solution.py:362
  16.0 11.3 %collective-permute-start.6 = (bf16[128,768]{1,0:T(8,128)(2,1)S(1)}, bf16[128,768]{1,0:T(8,128)(2,1)S(1)}, u32[]{:S(2)}, u32[]{:S(2)}) collective-permute-start(bf16[128,768]{1,0:T(8,128)(2,1)S(1)} %pad_maximum_fusion.refs_4_), channel_id=1, source_target_pairs={{0,2},{1,3},{2,0},{3,1},{4,6},{5,7},{6,4},{7,5},{8,10},{9,11},{10,... | collective-permute-start | bytes 589832 | tf_op jit(solution)/shard_map/ppermute | solution.py:362
  17.5 9.8 %collective-permute-start.5 = (bf16[128,768]{1,0:T(8,128)(2,1)S(1)}, bf16[128,768]{1,0:T(8,128)(2,1)S(1)}, u32[]{:S(2)}, u32[]{:S(2)}) collective-permute-start(bf16[128,768]{1,0:T(8,128)(2,1)S(1)} %collective-permute-done.4.refs_2_), channel_id=1, source_target_pairs={{0,4},{4,0},{8,12},{12,8},{16,20},{20,16},{24,28},{28,24},{1,5},{5... | collective-permute-start | bytes 589832 | tf_op jit(solution)/shard_map/ppermute | solution.py:362
  22.1 3.6 %collective-permute-start.16 = (s32[2,256]{1,0:T(2,128)S(1)}, s32[2,256]{1,0:T(2,128)S(1)}, u32[]{:S(2)}, u32[]{:S(2)}) collective-permute-start(s32[2,256]{1,0:T(2,128)S(1)} %pad_add_fusion.1), channel_id=1, source_target_pairs={{0,8},{4,12},{8,0},{12,4},{16,24},{20,28},{24,16},{28,20},{1,9},{5... | collective-permute-start | bytes 6152 | tf_op jit(solution)/shard_map/ppermute | solution.py:362
  22.1 5.7 %collective-permute-start.8 = (bf16[128,768]{1,0:T(8,128)(2,1)S(1)}, bf16[128,768]{1,0:T(8,128)(2,1)S(1)}, u32[]{:S(2)}, u32[]{:S(2)}) collective-permute-start(bf16[128,768]{1,0:T(8,128)(2,1)S(1)} %collective-permute-done.7.refs_6_), channel_id=1, source_target_pairs={{0,2},{1,3},{2,0},{3,1},{4,6},{5,7},{6,4},{7,5},{8,10},{9,11},{10,... | collective-permute-start | bytes 589832 | tf_op jit(solution)/shard_map/ppermute | solution.py:362
  25.7 4.5 %collective-permute-start.17 = (s32[4,256]{1,0:T(4,128)S(1)}, s32[4,256]{1,0:T(4,128)S(1)}, u32[]{:S(2)}, u32[]{:S(2)}) collective-permute-start(s32[4,256]{1,0:T(4,128)S(1)} %pad_add_fusion), channel_id=1, source_target_pairs={{0,16},{4,20},{8,24},{12,28},{16,0},{20,4},{24,8},{28,12},{1,17},{... | collective-permute-start | bytes 12296 | tf_op jit(solution)/shard_map/ppermute | solution.py:362
  27.8 3.0 %collective-permute-start.9 = (bf16[128,768]{1,0:T(8,128)(2,1)S(1)}, bf16[128,768]{1,0:T(8,128)(2,1)S(1)}, u32[]{:S(2)}, u32[]{:S(2)}) collective-permute-start(bf16[128,768]{1,0:T(8,128)(2,1)S(1)} %collective-permute-done.2.refs_1_), channel_id=1, source_target_pairs={{0,1},{1,0},{2,3},{3,2},{4,5},{5,4},{6,7},{7,6},{8,9},{9,8},{10,11... | collective-permute-start | bytes 589832 | tf_op jit(solution)/shard_map/ppermute | solution.py:362
  27.8 3.5 %collective-permute-start.10 = (bf16[128,768]{1,0:T(8,128)(2,1)S(1)}, bf16[128,768]{1,0:T(8,128)(2,1)S(1)}, u32[]{:S(2)}, u32[]{:S(2)}) collective-permute-start(bf16[128,768]{1,0:T(8,128)(2,1)S(1)} %collective-permute-done.4.refs_2_), channel_id=1, source_target_pairs={{0,1},{1,0},{2,3},{3,2},{4,5},{5,4},{6,7},{7,6},{8,9},{9,8},{10,11... | collective-permute-start | bytes 589832 | tf_op jit(solution)/shard_map/ppermute | solution.py:362
  30.3 1.4 %collective-permute-start.11 = (bf16[128,768]{1,0:T(8,128)(2,1)S(1)}, bf16[128,768]{1,0:T(8,128)(2,1)S(1)}, u32[]{:S(2)}, u32[]{:S(2)}) collective-permute-start(bf16[128,768]{1,0:T(8,128)(2,1)S(1)} %collective-permute-done.5.refs_3_), channel_id=1, source_target_pairs={{0,1},{1,0},{2,3},{3,2},{4,5},{5,4},{6,7},{7,6},{8,9},{9,8},{10,11... | collective-permute-start | bytes 589832 | tf_op jit(solution)/shard_map/ppermute | solution.py:362
  30.3 1.7 %collective-permute-start.12 = (bf16[128,768]{1,0:T(8,128)(2,1)S(1)}, bf16[128,768]{1,0:T(8,128)(2,1)S(1)}, u32[]{:S(2)}, u32[]{:S(2)}) collective-permute-start(bf16[128,768]{1,0:T(8,128)(2,1)S(1)} %pad_maximum_fusion.refs_4_), channel_id=1, source_target_pairs={{0,1},{1,0},{2,3},{3,2},{4,5},{5,4},{6,7},{7,6},{8,9},{9,8},{10,11... | collective-permute-start | bytes 589832 | tf_op jit(solution)/shard_map/ppermute | solution.py:362
  30.8 1.5 %collective-permute-start.13 = (bf16[128,768]{1,0:T(8,128)(2,1)S(1)}, bf16[128,768]{1,0:T(8,128)(2,1)S(1)}, u32[]{:S(2)}, u32[]{:S(2)}) collective-permute-start(bf16[128,768]{1,0:T(8,128)(2,1)S(1)} %collective-permute-done.6.refs_5_), channel_id=1, source_target_pairs={{0,1},{1,0},{2,3},{3,2},{4,5},{5,4},{6,7},{7,6},{8,9},{9,8},{10,11... | collective-permute-start | bytes 589832 | tf_op jit(solution)/shard_map/ppermute | solution.py:362
  30.8 1.7 %collective-permute-start.14 = (bf16[128,768]{1,0:T(8,128)(2,1)S(1)}, bf16[128,768]{1,0:T(8,128)(2,1)S(1)}, u32[]{:S(2)}, u32[]{:S(2)}) collective-permute-start(bf16[128,768]{1,0:T(8,128)(2,1)S(1)} %collective-permute-done.7.refs_6_), channel_id=1, source_target_pairs={{0,1},{1,0},{2,3},{3,2},{4,5},{5,4},{6,7},{7,6},{8,9},{9,8},{10,11... | collective-permute-start | bytes 589832 | tf_op jit(solution)/shard_map/ppermute | solution.py:362
  31.3 1.5 %collective-permute-start.15 = (bf16[128,768]{1,0:T(8,128)(2,1)S(1)}, bf16[128,768]{1,0:T(8,128)(2,1)S(1)}, u32[]{:S(2)}, u32[]{:S(2)}) collective-permute-start(bf16[128,768]{1,0:T(8,128)(2,1)S(1)} %collective-permute-done.8.refs_7_), channel_id=1, source_target_pairs={{0,1},{1,0},{2,3},{3,2},{4,5},{5,4},{6,7},{7,6},{8,9},{9,8},{10,11... | collective-permute-start | bytes 589832 | tf_op jit(solution)/shard_map/ppermute | solution.py:362
